TPU v7x, 32 devices: a whole 2x2x4 slice. The times are simulated.
32 devices in a mesh: group: 8 (over z, y), tp: 4 (over x, core).
Axes of the slice: x: 2, y: 2, z: 4, core: 2. Of those that a mesh axis runs over, the one named last changes fastest.
Arguments:
- pf_query: bfloat16 [2048, 8192], P('group', 'tp'), may hold values from -16 to 16
- pf_cache: bfloat16 [8, 2, 4096, 1024], P('group', None, 'tp'), may hold values from -16 to 16
- pf_offset: int32 [8], replicated, may hold values from 0 to 3840
- dec_query: bfloat16 [16, 8192], P('group', 'tp'), may hold values from -16 to 16
- dec_cache: bfloat16 [24, 2, 2048, 1024], P('group', None, 'tp'), may hold values from -16 to 16
- slot_owner: int32 [24], replicated, may hold values from 0 to 15, as said below
- slot_len: int32 [24], replicated, may hold values from 1 to 2048
Outputs:
- pf_out: bfloat16 [2048, 8192], P('group', 'tp')
- dec_out: bfloat16 [16, 8192], P('group', 'tp')
Inputs may be any that keep to these rules, and one draw needn't show every extreme that they name: `slot_owner`: every decode request owns one or two slots.
All inputs are finite; a program needn't handle non-finite values.
Results may differ from a plain program's by a relative error of at most 0.005.
Values may be sent and summed in bfloat16 or wider, within the bound.
A program may use at most 128 MiB of HBM per device.

v0:
```python
import jax
import jax.numpy as jnp
from jax import lax
from jax.sharding import PartitionSpec as P

QH = 64
KVH = 8
HD = 128
negative_big = -1e30


def merged_2(value, axis, join):
    pieces = jax.tree.map(lambda part: lax.all_gather(part, axis), value)
    head = jax.tree.map(lambda part: part[0], pieces)
    tail = jax.tree.map(lambda part: part[1:], pieces)
    running, _ = lax.scan(lambda running, share: (join(running, share), None), head, tail)
    return running


def attend_block(queries, cache_keys, cache_values, visible, score_scale):
    scores = (
        jnp.einsum("qgd,nd->gqn", queries, cache_keys, preferred_element_type=jnp.float32)
        * score_scale
    )
    scores = jnp.where(visible[None], scores, negative_big)
    maxima = jnp.max(scores, axis=-1)
    weights = jnp.where(visible[None], jnp.exp(scores - maxima[..., None]), 0.0).astype(
        jnp.bfloat16
    )
    totals = jnp.sum(weights, axis=-1, dtype=jnp.float32)
    weighted = jnp.einsum("gqn,nd->gqd", weights, cache_values, preferred_element_type=jnp.float32)
    return (maxima, totals, weighted)


def merge_along(maxima, totals, weighted, axis):
    largest = jnp.max(maxima, axis=axis, keepdims=True)
    factor = jnp.exp(maxima - largest)
    return (
        jnp.squeeze(largest, axis),
        jnp.sum(totals * factor, axis=axis),
        jnp.sum(weighted * factor[..., None], axis=axis),
    )


def combine_pair(first, second):
    largest = jnp.maximum(first[0], second[0])
    first_factor = jnp.exp(first[0] - largest)
    second_factor = jnp.exp(second[0] - largest)
    return (
        largest,
        first[1] * first_factor + second[1] * second_factor,
        first[2] * first_factor[..., None] + second[2] * second_factor[..., None],
    )


def masked_merge(hits, maxima, totals, weighted):
    selected_picks = jnp.where(hits[:, :, None], maxima[None], negative_big)
    largest = jnp.max(selected_picks, axis=1)
    factor = jnp.where(hits[:, :, None], jnp.exp(selected_picks - largest[:, None]), 0.0)
    denominator = jnp.einsum("abh,bh->ah", factor, totals, precision=lax.Precision.HIGHEST)
    numerator = jnp.einsum("abh,bhd->ahd", factor, weighted, precision=lax.Precision.HIGHEST)
    return (largest, denominator, numerator)


def on_device(pf_query, pf_cache, pf_offset, dec_query, dec_cache, slot_owner, slot_len):
    tp_count = lax.axis_size("tp")
    tp_rank = lax.axis_index("tp")
    group_rank = lax.axis_index("group")
    head_size = HD
    kv_heads = KVH
    width = QH // KVH
    local_heads = QH // tp_count
    score_scale = head_size ** (-0.5)
    pf_rows = pf_query.shape[0]
    local_len = pf_cache.shape[2]
    offset = lax.dynamic_index_in_dim(pf_offset, group_rank, keepdims=False)
    query_pos = offset + jnp.arange(pf_rows, dtype=jnp.int32)
    every_head = lax.all_gather(pf_query, "tp", axis=1, tiled=True)
    grouped = jnp.moveaxis(every_head.reshape(pf_rows, kv_heads, width, head_size), 1, 0)
    cache_keys = jnp.moveaxis(pf_cache[0, 0].reshape(local_len, kv_heads, head_size), 1, 0)
    cache_values = jnp.moveaxis(pf_cache[0, 1].reshape(local_len, kv_heads, head_size), 1, 0)
    key_pos = tp_rank * local_len + jnp.arange(local_len, dtype=jnp.int32)
    visible = key_pos[None, :] <= query_pos[:, None]
    maxima, totals, weighted = lax.map(
        lambda items: attend_block(items[0], items[1], items[2], visible, score_scale),
        (grouped, cache_keys, cache_values),
    )
    maxima = maxima.reshape(tp_count, local_heads, pf_rows)
    totals = totals.reshape(tp_count, local_heads, pf_rows)
    weighted = weighted.reshape(tp_count, local_heads, pf_rows, head_size)
    maxima, totals, weighted = (
        lax.all_to_all(maxima, "tp", split_axis=0, concat_axis=0, tiled=True),
        lax.all_to_all(totals, "tp", split_axis=0, concat_axis=0, tiled=True),
        lax.all_to_all(weighted, "tp", split_axis=0, concat_axis=0, tiled=True),
    )
    largest, denominator, numerator = merge_along(maxima, totals, weighted, 0)
    prefill_heads = numerator / denominator[..., None]
    pf_out = (
        jnp.moveaxis(prefill_heads, 1, 0)
        .reshape(pf_rows, local_heads * head_size)
        .astype(jnp.bfloat16)
    )
    served = dec_query.shape[0]
    head_queries_dec = lax.all_gather(dec_query, "tp", axis=1, tiled=True)
    all_queries = lax.all_gather(head_queries_dec, "group", axis=0, tiled=True)
    slots_here = dec_cache.shape[0]
    slot_local_len = dec_cache.shape[2]
    owners = lax.dynamic_slice_in_dim(slot_owner, group_rank * slots_here, slots_here)
    length_list = lax.dynamic_slice_in_dim(slot_len, group_rank * slots_here, slots_here)
    slot_queries = jnp.take(all_queries, owners, axis=0).reshape(
        slots_here, kv_heads, width, head_size
    )
    slot_keys = dec_cache[:, 0].reshape(slots_here, slot_local_len, kv_heads, head_size)
    slot_values = dec_cache[:, 1].reshape(slots_here, slot_local_len, kv_heads, head_size)
    scores = (
        jnp.einsum("skgd,slkd->skgl", slot_queries, slot_keys, preferred_element_type=jnp.float32)
        * score_scale
    )
    slot_pos = tp_rank * slot_local_len + jnp.arange(slot_local_len, dtype=jnp.int32)
    live = (slot_pos[None, :] < length_list[:, None])[:, None, None, :]
    scores = jnp.where(live, scores, negative_big)
    slot_max = jnp.max(scores, axis=-1)
    slot_weights = jnp.where(live, jnp.exp(scores - slot_max[..., None]), 0.0).astype(jnp.bfloat16)
    slot_totals = jnp.sum(slot_weights, axis=-1, dtype=jnp.float32)
    slot_weighted = jnp.einsum(
        "skgl,slkd->skgd", slot_weights, slot_values, preferred_element_type=jnp.float32
    )
    slot_max = slot_max.reshape(slots_here, QH)
    slot_totals = slot_totals.reshape(slots_here, QH)
    slot_weighted = slot_weighted.reshape(slots_here, QH, head_size)
    merged = merged_2((slot_max, slot_totals, slot_weighted), "tp", combine_pair)
    head_max = lax.dynamic_slice_in_dim(merged[0], tp_rank * local_heads, local_heads, 1)
    head_totals = lax.dynamic_slice_in_dim(merged[1], tp_rank * local_heads, local_heads, 1)
    head_weighted = lax.dynamic_slice_in_dim(merged[2], tp_rank * local_heads, local_heads, 1)
    every_max, every_totals, every_weighted = (
        lax.all_gather(head_max, "group", axis=0, tiled=True),
        lax.all_gather(head_totals, "group", axis=0, tiled=True),
        lax.all_gather(head_weighted, "group", axis=0, tiled=True),
    )
    mine = group_rank * served + jnp.arange(served, dtype=jnp.int32)
    hits = slot_owner[None, :] == mine[:, None]
    largest_dec, denominator_dec, numerator_dec = masked_merge(
        hits, every_max, every_totals, every_weighted
    )
    dec_out = (
        (numerator_dec / denominator_dec[..., None])
        .reshape(served, local_heads * head_size)
        .astype(jnp.bfloat16)
    )
    return (pf_out, dec_out)


def solution(mesh):
    placed = (
        P("group", "tp"),
        P("group", None, "tp", None),
        P(),
        P("group", "tp"),
        P("group", None, "tp", None),
        P(),
        P(),
    )
    return jax.shard_map(
        on_device,
        mesh=mesh,
        in_specs=placed,
        out_specs=(P("group", "tp"), P("group", "tp")),
        check_vma=False,
    )
```

profile of v0, /device:TPU:0, one launch (start us, length us, event | category | flops | bytes accessed | tf_op | source)
XLA Modules:
  0.0 403.5 jit_solution(4472428663473686276)
XLA Ops:
  7.2 2.3 copy.40
  9.5 4.0 fusion.46
  13.5 4.0 copy.61
  17.5 2.6 copy.62
  21.2 26.1 %all-gather.5.cloned.1.call-done = bf16[256,8192]{0,1:T(8,128)(2,1)} async-done(((bf16[256,2048]{0,1:T(8,128)(2,1)}), bf16[256,8192]{0,1:T(8,128)(2,1)}) %all-gather.5.cloned.1.call-update) | async-done | bytes 4194320 | tf_op jit(solution)/shard_map/all_gather | solution.py:78
  47.3 74.8 %while.30 = (s32[]{:T(128)}, f32[8,8,256]{2,1,0:T(8,128)S(1)}, f32[8,8,256]{2,1,0:T(8,128)S(1)}, f32[8,8,256,128]{3,2,1,0:T(8,128)}, bf16[8,1024,128]{1,2,0:T(8,...) while((s32[]{:T(128)}, f32[8,8,256]{2,1,0:T(8,128)S(1)}, ...), condition=%wide.region_3.4_spmd.clone, body=%wide.region_0.3_spmd.clone.sunk | while | flops 1105457152 | bytes 28384368 | solution.py:84
  47.6 2.6 fusion.59
  50.2 2.0 convert_reduce_fusion.3
  52.2 4.6 %fusion.60 = f32[8,8,256,128]{3,2,1,0:T(8,128)} fusion(f32[8,8,256,128]{3,2,1,0:T(8,128)} %get-tuple-element.319, s32[]{:T(128)S(6)} %copy.81, bf16[8,1024,128]{1,2,0:T(8,128)(2,1)} %get-tuple-element.332, f32[1024,256,8]{1,0,2:T(8,128)S(1)} %get-tuple-element.303, f32[8,256]{1,0:T(8,128)S(1)} %get-tuple-element.302, ...), kind=kOutput, calls=%fused_computation.15.clone.1 | convolution fusion | flops 547356672 | bytes 9970688 | tf_op jit(solution)/shard_map/while/body/eval_jaxpr/gqn,nd->gqd/dot_general | solution.py:31
  57.0 2.6 fusion.59
  59.6 2.0 convert_reduce_fusion.3
  61.6 4.5 %fusion.60 = f32[8,8,256,128]{3,2,1,0:T(8,128)} fusion(f32[8,8,256,128]{3,2,1,0:T(8,128)} %get-tuple-element.319, s32[]{:T(128)S(6)} %copy.81, bf16[8,1024,128]{1,2,0:T(8,128)(2,1)} %get-tuple-element.332, f32[1024,256,8]{1,0,2:T(8,128)S(1)} %get-tuple-element.303, f32[8,256]{1,0:T(8,128)S(1)} %get-tuple-element.302, ...), kind=kOutput, calls=%fused_computation.15.clone.1 | convolution fusion | flops 547356672 | bytes 9970688 | tf_op jit(solution)/shard_map/while/body/eval_jaxpr/gqn,nd->gqd/dot_general | solution.py:31
  66.3 2.6 fusion.59
  68.9 2.0 convert_reduce_fusion.3
  70.9 4.5 %fusion.60 = f32[8,8,256,128]{3,2,1,0:T(8,128)} fusion(f32[8,8,256,128]{3,2,1,0:T(8,128)} %get-tuple-element.319, s32[]{:T(128)S(6)} %copy.81, bf16[8,1024,128]{1,2,0:T(8,128)(2,1)} %get-tuple-element.332, f32[1024,256,8]{1,0,2:T(8,128)S(1)} %get-tuple-element.303, f32[8,256]{1,0:T(8,128)S(1)} %get-tuple-element.302, ...), kind=kOutput, calls=%fused_computation.15.clone.1 | convolution fusion | flops 547356672 | bytes 9970688 | tf_op jit(solution)/shard_map/while/body/eval_jaxpr/gqn,nd->gqd/dot_general | solution.py:31
  75.6 2.6 fusion.59
  78.2 2.0 convert_reduce_fusion.3
  80.3 4.5 %fusion.60 = f32[8,8,256,128]{3,2,1,0:T(8,128)} fusion(f32[8,8,256,128]{3,2,1,0:T(8,128)} %get-tuple-element.319, s32[]{:T(128)S(6)} %copy.81, bf16[8,1024,128]{1,2,0:T(8,128)(2,1)} %get-tuple-element.332, f32[1024,256,8]{1,0,2:T(8,128)S(1)} %get-tuple-element.303, f32[8,256]{1,0:T(8,128)S(1)} %get-tuple-element.302, ...), kind=kOutput, calls=%fused_computation.15.clone.1 | convolution fusion | flops 547356672 | bytes 9970688 | tf_op jit(solution)/shard_map/while/body/eval_jaxpr/gqn,nd->gqd/dot_general | solution.py:31
  84.9 2.6 fusion.59
  87.5 2.0 convert_reduce_fusion.3
  89.6 4.5 %fusion.60 = f32[8,8,256,128]{3,2,1,0:T(8,128)} fusion(f32[8,8,256,128]{3,2,1,0:T(8,128)} %get-tuple-element.319, s32[]{:T(128)S(6)} %copy.81, bf16[8,1024,128]{1,2,0:T(8,128)(2,1)} %get-tuple-element.332, f32[1024,256,8]{1,0,2:T(8,128)S(1)} %get-tuple-element.303, f32[8,256]{1,0:T(8,128)S(1)} %get-tuple-element.302, ...), kind=kOutput, calls=%fused_computation.15.clone.1 | convolution fusion | flops 547356672 | bytes 9970688 | tf_op jit(solution)/shard_map/while/body/eval_jaxpr/gqn,nd->gqd/dot_general | solution.py:31
  94.3 2.6 fusion.59
  96.9 2.0 convert_reduce_fusion.3
  99.0 4.5 %fusion.60 = f32[8,8,256,128]{3,2,1,0:T(8,128)} fusion(f32[8,8,256,128]{3,2,1,0:T(8,128)} %get-tuple-element.319, s32[]{:T(128)S(6)} %copy.81, bf16[8,1024,128]{1,2,0:T(8,128)(2,1)} %get-tuple-element.332, f32[1024,256,8]{1,0,2:T(8,128)S(1)} %get-tuple-element.303, f32[8,256]{1,0:T(8,128)S(1)} %get-tuple-element.302, ...), kind=kOutput, calls=%fused_computation.15.clone.1 | convolution fusion | flops 547356672 | bytes 9970688 | tf_op jit(solution)/shard_map/while/body/eval_jaxpr/gqn,nd->gqd/dot_general | solution.py:31
  103.7 2.6 fusion.59
  106.3 2.0 convert_reduce_fusion.3
  108.3 4.5 %fusion.60 = f32[8,8,256,128]{3,2,1,0:T(8,128)} fusion(f32[8,8,256,128]{3,2,1,0:T(8,128)} %get-tuple-element.319, s32[]{:T(128)S(6)} %copy.81, bf16[8,1024,128]{1,2,0:T(8,128)(2,1)} %get-tuple-element.332, f32[1024,256,8]{1,0,2:T(8,128)S(1)} %get-tuple-element.303, f32[8,256]{1,0:T(8,128)S(1)} %get-tuple-element.302, ...), kind=kOutput, calls=%fused_computation.15.clone.1 | convolution fusion | flops 547356672 | bytes 9970688 | tf_op jit(solution)/shard_map/while/body/eval_jaxpr/gqn,nd->gqd/dot_general | solution.py:31
  113.0 2.6 fusion.59
  115.6 2.0 convert_reduce_fusion.3
  117.6 4.5 %fusion.60 = f32[8,8,256,128]{3,2,1,0:T(8,128)} fusion(f32[8,8,256,128]{3,2,1,0:T(8,128)} %get-tuple-element.319, s32[]{:T(128)S(6)} %copy.81, bf16[8,1024,128]{1,2,0:T(8,128)(2,1)} %get-tuple-element.332, f32[1024,256,8]{1,0,2:T(8,128)S(1)} %get-tuple-element.303, f32[8,256]{1,0:T(8,128)S(1)} %get-tuple-element.302, ...), kind=kOutput, calls=%fused_computation.15.clone.1 | convolution fusion | flops 547356672 | bytes 9970688 | tf_op jit(solution)/shard_map/while/body/eval_jaxpr/gqn,nd->gqd/dot_general | solution.py:31
  122.1 7.1 %all_to_all.15 = f32[4,16,256]{2,1,0:T(8,128)} all-to-all(f32[4,16,256]{2,1,0:T(8,128)S(1)} %bitcast.139), channel_id=1, replica_groups=mesh['group'=8,'tp'=4] {'tp'}, dimensions={0} | all-to-all | bytes 131072 | tf_op jit(solution)/shard_map/all_to_all | solution.py:93
  129.2 7.1 %all_to_all.16 = f32[4,16,256]{2,1,0:T(8,128)} all-to-all(f32[4,16,256]{2,1,0:T(8,128)S(1)} %bitcast.138), channel_id=1, replica_groups=mesh['group'=8,'tp'=4] {'tp'}, dimensions={0} | all-to-all | bytes 131072 | tf_op jit(solution)/shard_map/all_to_all | solution.py:92
  136.4 5.7 %all-to-all-start = ((f32[4,16,256,128]{3,2,1,0:T(8,128)}), f32[4,16,256,128]{3,2,1,0:T(8,128)}, u32[]{:S(2)}, u32[]{:S(2)}) async-start(f32[4,16,256,128]{3,2,1,0:T(8,128)} %bitcast.130), calls=%async_computation | async-start | bytes 16777216 | tf_op jit(solution)/shard_map/all_to_all | solution.py:94
  142.1 6.9 %fusion.45 = (bf16[3,1,512,1024]{3,2,1,0:T(8,128)(2,1)}, bf16[3,1,512,1024]{3,2,1,0:T(8,128)(2,1)}) fusion(bf16[3,2,512,1024]{3,2,1,0:T(8,128)(2,1)} %param.15), kind=kLoop, calls=%fused_computation.81 | loop fusion | bytes 12582912 | tf_op jit(solution)/shard_map/slice | solution.py:114
  149.0 3.2 copy.63
  152.2 84.0 %all_gather.28 = bf16[2,8192]{1,0:T(2,128)(2,1)S(1)} all-gather(bf16[2,2048]{1,0:T(2,128)(2,1)S(1)} %copy-done.2), channel_id=1, replica_groups=mesh['group'=8,'tp'=4] {'tp'}, dimensions={1}, use_global_device_ids=true | all-gather | bytes 40960 | tf_op jit(solution)/shard_map/all_gather | solution.py:104
  236.2 32.8 %all-gather = bf16[8,2,8192]{2,1,0:T(2,128)(2,1)} all-gather(bf16[1,2,8192]{2,1,0:T(2,128)(2,1)S(1)} %bitcast.136), channel_id=1, replica_groups=mesh['group'=8,'tp'=4] {'group'}, dimensions={0}, use_global_device_ids=true | all-gather | bytes 294912 | tf_op jit(solution)/shard_map/all_gather | solution.py:105
  269.0 1.0 reshape.122
  270.7 1.2 gather_fusion
  272.0 1.5 fusion.47
  273.5 0.7 all_gather_reshape.9
  274.4 0.7 all_gather_reshape.10
  275.1 3.2 copy.64
  278.3 5.3 %all_gather.30 = f32[4,3,64]{2,1,0:T(4,128)S(1)} all-gather(f32[1,3,64]{2,1,0:T(4,128)} %all_gather_reshape.9), channel_id=1, replica_groups=mesh['group'=8,'tp'=4] {'tp'}, dimensions={0}, use_global_device_ids=true | all-gather | bytes 3840 | tf_op jit(solution)/shard_map/all_gather | solution.py:13
  284.2 5.3 %all_gather.31 = f32[4,3,64]{2,1,0:T(4,128)S(1)} all-gather(f32[1,3,64]{2,1,0:T(4,128)} %all_gather_reshape.10), channel_id=1, replica_groups=mesh['group'=8,'tp'=4] {'tp'}, dimensions={0}, use_global_device_ids=true | all-gather | bytes 3840 | tf_op jit(solution)/shard_map/all_gather | solution.py:13
  289.4 0.6 slice.46
  290.0 1.0 convolution_bitcast_fusion.1
  291.0 6.5 %all_gather.32 = f32[4,3,64,128]{3,2,1,0:T(8,128)S(1)} all-gather(f32[1,3,64,128]{3,2,1,0:T(8,128)S(1)} %convolution_bitcast_fusion.1), channel_id=1, replica_groups=mesh['group'=8,'tp'=4] {'tp'}, dimensions={0}, use_global_device_ids=true | all-gather | bytes 491520 | tf_op jit(solution)/shard_map/all_gather | solution.py:13
  297.6 0.7 slice_bitcast_fusion.2
  298.3 0.7 slice_bitcast_fusion.1
  298.9 2.6 while.29
  299.0 0.7 fusion.56
  299.8 0.7 fusion.56
  300.7 0.7 fusion.56
  301.6 26.0 %all-gather.2 = f32[8,3,16]{2,1,0:T(4,128)S(1)} all-gather(f32[1,3,16]{2,1,0:T(4,128)S(1)} %dynamic-slice_bitcast_fusion), channel_id=1, replica_groups=mesh['group'=8,'tp'=4] {'group'}, dimensions={0}, use_global_device_ids=true | all-gather | bytes 1728 | tf_op jit(solution)/shard_map/all_gather | solution.py:137
  327.8 26.2 %all-gather.1 = f32[8,3,16]{2,1,0:T(4,128)S(1)} all-gather(f32[1,3,16]{2,1,0:T(4,128)S(1)} %dynamic-slice_bitcast_fusion.1), channel_id=1, replica_groups=mesh['group'=8,'tp'=4] {'group'}, dimensions={0}, use_global_device_ids=true | all-gather | bytes 1728 | tf_op jit(solution)/shard_map/all_gather | solution.py:136
  354.0 30.6 %all_gather.33 = f32[24,16,128]{2,1,0:T(8,128)S(1)} all-gather(f32[3,16,128]{2,1,0:T(8,128)S(1)} %constant_dynamic-slice_fusion), channel_id=1, replica_groups=mesh['group'=8,'tp'=4] {'group'}, dimensions={0}, use_global_device_ids=true | all-gather | bytes 221184 | tf_op jit(solution)/shard_map/all_gather | solution.py:138
  384.7 0.7 broadcast_compare_fusion.2
  385.8 1.0 fusion.20
  386.8 0.8 reduce_max.36
  387.6 0.9 multiply_reduce_fusion.1
  388.5 5.4 %multiply_reduce_fusion = f32[16,256,128]{2,1,0:T(8,128)S(1)} fusion(f32[4,16,256,128]{3,2,1,0:T(8,128)} %all-to-all-done, f32[4,16,256]{2,1,0:T(8,128)S(1)} %get-tuple-element.181), kind=kLoop, calls=%fused_computation.28 | loop fusion | flops 3670016 | bytes 10551296 | tf_op jit(solution)/shard_map/reduce_sum | solution.py:41
  393.9 0.7 fusion.16
  395.2 1.4 copy.52
  (60 shorter events, 6.2 us)
Async XLA Ops:
  7.2 40.2 %all-gather.5.cloned.1.call-start = ((), (), s32[]{:S(2)}) async-start(), calls=%async_computation.3 | async-start | bytes 5242880 | tf_op jit(solution)/shard_map/all_gather | solution.py:78
  13.5 6.5 %copy-start.4 = (s32[8]{0:T(128)S(1)}, s32[8]{0:T(128)}, u32[]{:S(2)}) copy-start(s32[8]{0:T(128)} %param.13) | copy-start | bytes 100
  136.4 252.1 %all-to-all-start = ((f32[4,16,256,128]{3,2,1,0:T(8,128)}), f32[4,16,256,128]{3,2,1,0:T(8,128)}, u32[]{:S(2)}, u32[]{:S(2)}) async-start(f32[4,16,256,128]{3,2,1,0:T(8,128)} %bitcast.130), calls=%async_computation | async-start | bytes 16777216 | tf_op jit(solution)/shard_map/all_to_all | solution.py:94
  149.0 3.2 copy-start.2
  149.0 121.1 %copy-start.5 = (s32[24]{0:T(128)S(1)}, s32[24]{0:T(128)}, u32[]{:S(2)}) copy-start(s32[24]{0:T(128)} %param.17) | copy-start | bytes 292
  149.0 121.2 %copy-start.3 = (s32[24]{0:T(128)S(1)}, s32[24]{0:T(128)}, u32[]{:S(2)}) copy-start(s32[24]{0:T(128)} %param.16) | copy-start | bytes 292
  283.6 6.5 %copy-start = (f32[4,3,64]{2,1,0:T(4,128)}, f32[4,3,64]{2,1,0:T(4,128)S(1)}, u32[]{:S(2)}) copy-start(f32[4,3,64]{2,1,0:T(4,128)S(1)} %all_gather.30) | copy-start | bytes 9220
  289.4 0.6 copy-start.1
Sparse Core Ops, SparseCore 0:
  10.1 37.1 all-gather.4
where the time goes:
time: 405 us; the launch traced here: 403 us
  blocking collectives  231 us (57%)
  matrix products  60.3 us (15%)
  local copies, waits for them, and re-layouts  35.3 us (9%)
  other arithmetic  30.4 us (8%)
  waiting for transfers between devices  26.1 us (6%)
  between operations  14.2 us (4%)
  starting transfers between devices  5.69 us (1%)
    all_gather x1, blocking collectives, on_device(): head_queries_dec = lax.all_gather(dec_query, 'tp', axis=1, tiled=True)  84 us
    dot_general x8, matrix products, attend_block(): jnp.einsum('gqn,nd->gqd', weights, cache_values, preferred_element_type=j...  35.9 us
    all_gather x1, blocking collectives, on_device(): all_queries = lax.all_gather(head_queries_dec, 'group', axis=0, tiled=True)  32.8 us
    all_gather x1, blocking collectives, on_device(): lax.all_gather(head_weighted, 'group', axis=0, tiled=True)  30.6 us
    all_gather x1, blocking collectives, on_device(): lax.all_gather(head_max, 'group', axis=0, tiled=True)  26.2 us
    all_gather x1, waiting for transfers between devices, on_device(): every_head = lax.all_gather(pf_query, 'tp', axis=1, tiled=True)  26.1 us
    all_gather x1, blocking collectives, on_device(): lax.all_gather(head_totals, 'group', axis=0, tiled=True)  26 us
    dot_general x8, matrix products, attend_block(): jnp.einsum('qgd,nd->gqn', queries, cache_keys, preferred_element_type=jnp...  20.8 us
  transfers between devices with their start and end apart: 2, of which 1 were waited for; matrix products, arithmetic and copies ran while one was open for 10% of the time, Pallas kernels for 0%

commit v1 on v0

--- a/solution.py
+++ b/solution.py
@@ -102,7 +102,27 @@
     )
     served = dec_query.shape[0]
     head_queries_dec = lax.all_gather(dec_query, "tp", axis=1, tiled=True)
-    all_queries = lax.all_gather(head_queries_dec, "group", axis=0, tiled=True)
+
+    def drive_wires_for(message, net_axis):
+        full_n = lax.axis_size(net_axis)
+        mat_out = range(full_n)
+        plain = map(lambda w: (w, (w + 1) % full_n), mat_out)
+        pages = list(plain)
+        k_now = range(full_n)
+        t1 = map(lambda w: (w, (w - 1) % full_n), k_now)
+        line_up = list(t1)
+        ready, z2 = ([message], [message])
+        for _ in range(full_n // 2):
+            state_now = lax.ppermute(ready[-1], net_axis, pages)
+            ready.append(state_now)
+        for _ in [*range((full_n - 1) // 2)]:
+            v_now = lax.ppermute(z2[-1], net_axis, line_up)
+            z2.append(v_now)
+        high = jnp.concatenate([*ready[::-1], *z2[1:]], axis=0)
+        tmp = lax.axis_index(net_axis)
+        return jnp.roll(high, shift=(tmp - full_n // 2) * message.shape[0], axis=0)
+
+    all_queries = drive_wires_for(head_queries_dec, "group")
     slots_here = dec_cache.shape[0]
     slot_local_len = dec_cache.shape[2]
     owners = lax.dynamic_slice_in_dim(slot_owner, group_rank * slots_here, slots_here)

time: 405 us -> 365 us (0.901)
  blocking collectives: 231 us -> 165 us
  starting transfers between devices: 5.69 us -> 23.2 us
  local copies, waits for them, and re-layouts: 35.3 us -> 41.9 us
    all_gather x1, blocking collectives: 84 us -> 5.25 us  [on_device(): head_queries_dec = lax.all_gather(dec_query, 'tp', axis=1, tiled=True)]
    all_gather x3, blocking collectives: 17.1 us -> 70.2 us  [merged_2(): pieces = jax.tree.map(lambda part: lax.all_gather(part, axis), value)]
    all_gather x1 -> x0, blocking collectives: 32.8 us -> none  [on_device(): all_queries = lax.all_gather(head_queries_dec, 'group', axis=0, tiled=True)]
    ppermute x0 -> x7, starting transfers between devices: none -> 14.2 us  [the longest x3 12.7 us: drive_wires_for(): v_now = lax.ppermute(z2[-1], net_axis, line_up)]
    all_to_all x1 -> x0, blocking collectives: 7.15 us -> none  [on_device(): lax.all_to_all(maxima, 'tp', split_axis=0, concat_axis=0, tiled=True)]
    dynamic_update_slice x8, local copies, waits for them, and re-layouts: 0.07 us -> 4.82 us  [on_device(): lax.map(lambda items: attend_block(items[0], items[1], items[2], visible,...]
    unnamed x25 -> x28, local copies, waits for them, and re-layouts: 18 us -> 19.1 us
  transfers between devices with their start and end apart: 2 -> 10, of which waited for: 1 -> 3; matrix products, arithmetic and copies ran while one was open for 10% -> 12% of each run, Pallas kernels for 0% -> 0%
where the time goes in v1:
time: 365 us; the launch traced here: 363 us
  blocking collectives  165 us (45%)
  matrix products  62.8 us (17%)
  local copies, waits for them, and re-layouts  41.9 us (11%)
  waiting for transfers between devices  28.5 us (8%)
  other arithmetic  27.3 us (7%)
  starting transfers between devices  23.2 us (6%)
  between operations  14.3 us (4%)
    all_gather x3, blocking collectives, merged_2(): pieces = jax.tree.map(lambda part: lax.all_gather(part, axis), value)  70.2 us
    dot_general x8, matrix products, attend_block(): jnp.einsum('gqn,nd->gqd', weights, cache_values, preferred_element_type=j...  35.8 us
    all_gather x1, blocking collectives, on_device(): lax.all_gather(head_weighted, 'group', axis=0, tiled=True)  30.6 us
    all_gather x1, blocking collectives, on_device(): lax.all_gather(head_max, 'group', axis=0, tiled=True)  26 us
    all_gather x1, blocking collectives, on_device(): lax.all_gather(head_totals, 'group', axis=0, tiled=True)  26 us
    all_gather x1, waiting for transfers between devices, on_device(): every_head = lax.all_gather(pf_query, 'tp', axis=1, tiled=True)  26 us
    dot_general x8, matrix products, attend_block(): jnp.einsum('qgd,nd->gqn', queries, cache_keys, preferred_element_type=jnp...  20.8 us
    unnamed x28, local copies, waits for them, and re-layouts  19.1 us
  transfers between devices with their start and end apart: 10, of which 3 were waited for; matrix products, arithmetic and copies ran while one was open for 12% of the time, Pallas kernels for 0%

profile of v1, /device:TPU:0, one launch (start us, length us, event | category | flops | bytes accessed | tf_op | source)
XLA Modules:
  0.0 363.4 jit_solution(15378846371170492901)
XLA Ops:
  7.2 2.3 copy.40
  9.5 4.0 %fusion.46 = (bf16[1,1,1024,1024]{3,2,1,0:T(8,128)(2,1)S(1)}, bf16[1,1,1024,1024]{3,2,1,0:T(8,128)(2,1)}) fusion(bf16[1,2,1024,1024]{3,2,1,0:T(8,128)(2,1)} %param.12), kind=kLoop, calls=%fused_computation.83 | loop fusion | bytes 8388608 | tf_op jit(solution)/shard_map/slice | solution.py:81
  13.6 3.9 %copy.61 = bf16[1,1,1024,1024]{2,3,1,0:T(8,128)(2,1)} copy(bf16[1,1,1024,1024]{3,2,1,0:T(8,128)(2,1)} %get-tuple-element.189) | data formatting | bytes 4194304
  17.5 2.6 copy.62
  20.1 0.6 dynamic_slice.45
  20.7 0.6 iota_add_fusion.2
  21.4 26.0 %all-gather.4.cloned.1.call-done = bf16[256,8192]{0,1:T(8,128)(2,1)} async-done(((bf16[256,2048]{0,1:T(8,128)(2,1)}), bf16[256,8192]{0,1:T(8,128)(2,1)}) %all-gather.4.cloned.1.call-update) | async-done | bytes 4194320 | tf_op jit(solution)/shard_map/all_gather | solution.py:78
  47.3 79.4 %while.30 = (s32[]{:T(128)}, f32[8,8,256]{2,1,0:T(8,128)}, f32[8,8,256]{2,1,0:T(8,128)S(1)}, f32[8,8,256,128]{3,2,1,0:T(8,128)}, bf16[8,1024,128]{1,2,0:T(8,128)...) while((s32[]{:T(128)}, f32[8,8,256]{2,1,0:T(8,128)}, ...), condition=%wide.region_3.4_spmd.clone, body=%wide.region_0.3_spmd.clone.sunk | while | flops 1105457152 | bytes 28384368 | solution.py:84
  47.6 2.6 fusion.59
  50.2 2.0 convert_reduce_fusion.3
  52.8 4.5 %fusion.60 = f32[8,8,256,128]{3,2,1,0:T(8,128)} fusion(f32[8,8,256,128]{3,2,1,0:T(8,128)} %get-tuple-element.319, s32[]{:T(128)S(6)} %copy.81, bf16[8,1024,128]{1,2,0:T(8,128)(2,1)} %get-tuple-element.332, f32[1024,256,8]{1,0,2:T(8,128)S(1)} %get-tuple-element.303, f32[8,256]{1,0:T(8,128)S(1)} %get-tuple-element.302, ...), kind=kOutput, calls=%fused_computation.15.clone.1 | convolution fusion | flops 547356672 | bytes 9970688 | tf_op jit(solution)/shard_map/while/body/eval_jaxpr/gqn,nd->gqd/dot_general | solution.py:31
  57.5 2.6 fusion.59
  60.1 2.0 convert_reduce_fusion.3
  62.8 4.4 %fusion.60 = f32[8,8,256,128]{3,2,1,0:T(8,128)} fusion(f32[8,8,256,128]{3,2,1,0:T(8,128)} %get-tuple-element.319, s32[]{:T(128)S(6)} %copy.81, bf16[8,1024,128]{1,2,0:T(8,128)(2,1)} %get-tuple-element.332, f32[1024,256,8]{1,0,2:T(8,128)S(1)} %get-tuple-element.303, f32[8,256]{1,0:T(8,128)S(1)} %get-tuple-element.302, ...), kind=kOutput, calls=%fused_computation.15.clone.1 | convolution fusion | flops 547356672 | bytes 9970688 | tf_op jit(solution)/shard_map/while/body/eval_jaxpr/gqn,nd->gqd/dot_general | solution.py:31
  67.4 2.6 fusion.59
  70.0 2.0 convert_reduce_fusion.3
  72.7 4.5 %fusion.60 = f32[8,8,256,128]{3,2,1,0:T(8,128)} fusion(f32[8,8,256,128]{3,2,1,0:T(8,128)} %get-tuple-element.319, s32[]{:T(128)S(6)} %copy.81, bf16[8,1024,128]{1,2,0:T(8,128)(2,1)} %get-tuple-element.332, f32[1024,256,8]{1,0,2:T(8,128)S(1)} %get-tuple-element.303, f32[8,256]{1,0:T(8,128)S(1)} %get-tuple-element.302, ...), kind=kOutput, calls=%fused_computation.15.clone.1 | convolution fusion | flops 547356672 | bytes 9970688 | tf_op jit(solution)/shard_map/while/body/eval_jaxpr/gqn,nd->gqd/dot_general | solution.py:31
  77.3 2.6 fusion.59
  79.9 2.0 convert_reduce_fusion.3
  82.6 4.5 %fusion.60 = f32[8,8,256,128]{3,2,1,0:T(8,128)} fusion(f32[8,8,256,128]{3,2,1,0:T(8,128)} %get-tuple-element.319, s32[]{:T(128)S(6)} %copy.81, bf16[8,1024,128]{1,2,0:T(8,128)(2,1)} %get-tuple-element.332, f32[1024,256,8]{1,0,2:T(8,128)S(1)} %get-tuple-element.303, f32[8,256]{1,0:T(8,128)S(1)} %get-tuple-element.302, ...), kind=kOutput, calls=%fused_computation.15.clone.1 | convolution fusion | flops 547356672 | bytes 9970688 | tf_op jit(solution)/shard_map/while/body/eval_jaxpr/gqn,nd->gqd/dot_general | solution.py:31
  87.2 2.6 fusion.59
  89.8 2.0 convert_reduce_fusion.3
  91.9 0.6 bitcast_dynamic-update-slice_fusion.3
  92.5 4.5 %fusion.60 = f32[8,8,256,128]{3,2,1,0:T(8,128)} fusion(f32[8,8,256,128]{3,2,1,0:T(8,128)} %get-tuple-element.319, s32[]{:T(128)S(6)} %copy.81, bf16[8,1024,128]{1,2,0:T(8,128)(2,1)} %get-tuple-element.332, f32[1024,256,8]{1,0,2:T(8,128)S(1)} %get-tuple-element.303, f32[8,256]{1,0:T(8,128)S(1)} %get-tuple-element.302, ...), kind=kOutput, calls=%fused_computation.15.clone.1 | convolution fusion | flops 547356672 | bytes 9970688 | tf_op jit(solution)/shard_map/while/body/eval_jaxpr/gqn,nd->gqd/dot_general | solution.py:31
  97.2 2.6 fusion.59
  99.8 2.0 convert_reduce_fusion.3
  102.4 4.5 %fusion.60 = f32[8,8,256,128]{3,2,1,0:T(8,128)} fusion(f32[8,8,256,128]{3,2,1,0:T(8,128)} %get-tuple-element.319, s32[]{:T(128)S(6)} %copy.81, bf16[8,1024,128]{1,2,0:T(8,128)(2,1)} %get-tuple-element.332, f32[1024,256,8]{1,0,2:T(8,128)S(1)} %get-tuple-element.303, f32[8,256]{1,0:T(8,128)S(1)} %get-tuple-element.302, ...), kind=kOutput, calls=%fused_computation.15.clone.1 | convolution fusion | flops 547356672 | bytes 9970688 | tf_op jit(solution)/shard_map/while/body/eval_jaxpr/gqn,nd->gqd/dot_general | solution.py:31
  107.1 2.6 fusion.59
  109.7 2.0 convert_reduce_fusion.3
  112.3 4.5 %fusion.60 = f32[8,8,256,128]{3,2,1,0:T(8,128)} fusion(f32[8,8,256,128]{3,2,1,0:T(8,128)} %get-tuple-element.319, s32[]{:T(128)S(6)} %copy.81, bf16[8,1024,128]{1,2,0:T(8,128)(2,1)} %get-tuple-element.332, f32[1024,256,8]{1,0,2:T(8,128)S(1)} %get-tuple-element.303, f32[8,256]{1,0:T(8,128)S(1)} %get-tuple-element.302, ...), kind=kOutput, calls=%fused_computation.15.clone.1 | convolution fusion | flops 547356672 | bytes 9970688 | tf_op jit(solution)/shard_map/while/body/eval_jaxpr/gqn,nd->gqd/dot_general | solution.py:31
  117.0 2.6 fusion.59
  119.6 2.0 convert_reduce_fusion.3
  122.3 4.5 %fusion.60 = f32[8,8,256,128]{3,2,1,0:T(8,128)} fusion(f32[8,8,256,128]{3,2,1,0:T(8,128)} %get-tuple-element.319, s32[]{:T(128)S(6)} %copy.81, bf16[8,1024,128]{1,2,0:T(8,128)(2,1)} %get-tuple-element.332, f32[1024,256,8]{1,0,2:T(8,128)S(1)} %get-tuple-element.303, f32[8,256]{1,0:T(8,128)S(1)} %get-tuple-element.302, ...), kind=kOutput, calls=%fused_computation.15.clone.1 | convolution fusion | flops 547356672 | bytes 9970688 | tf_op jit(solution)/shard_map/while/body/eval_jaxpr/gqn,nd->gqd/dot_general | solution.py:31
  126.7 7.1 %all_to_all.15 = f32[4,16,256]{2,1,0:T(8,128)} all-to-all(f32[4,16,256]{2,1,0:T(8,128)S(1)} %bitcast.136), channel_id=1, replica_groups=mesh['group'=8,'tp'=4] {'tp'}, dimensions={0} | all-to-all | bytes 131072 | tf_op jit(solution)/shard_map/all_to_all | solution.py:93
  133.9 3.3 all-to-all-start.1
  137.2 5.3 %all_gather.25 = bf16[2,8192]{1,0:T(2,128)(2,1)S(1)} all-gather(bf16[2,2048]{1,0:T(2,128)(2,1)S(1)} %copy-done.3), channel_id=1, replica_groups=mesh['group'=8,'tp'=4] {'tp'}, dimensions={1}, use_global_device_ids=true | all-gather | bytes 40960 | tf_op jit(solution)/shard_map/all_gather | solution.py:104
  142.4 1.5 collective-permute-start
  143.9 3.2 collective-permute-start.4
  147.2 0.6 copy-done
  147.8 5.6 %all-to-all-start = ((f32[4,16,256,128]{3,2,1,0:T(8,128)}), f32[4,16,256,128]{3,2,1,0:T(8,128)}, u32[]{:S(2)}, u32[]{:S(2)}) async-start(f32[4,16,256,128]{3,2,1,0:T(8,128)} %bitcast.129), calls=%async_computation | async-start | bytes 16777216 | tf_op jit(solution)/shard_map/all_to_all | solution.py:94
  153.6 6.9 %fusion.45 = (bf16[3,1,512,1024]{3,2,1,0:T(8,128)(2,1)}, bf16[3,1,512,1024]{3,2,1,0:T(8,128)(2,1)}) fusion(bf16[3,2,512,1024]{3,2,1,0:T(8,128)(2,1)} %param.15), kind=kLoop, calls=%fused_computation.82 | loop fusion | bytes 12582912 | tf_op jit(solution)/shard_map/slice | solution.py:134
  161.2 4.7 %collective-permute-start.5 = (bf16[2,8192]{1,0:T(2,128)(2,1)S(1)}, bf16[2,8192]{1,0:T(2,128)(2,1)S(1)}, u32[]{:S(2)}, u32[]{:S(2)}) collective-permute-start(bf16[2,8192]{1,0:T(2,128)(2,1)S(1)} %collective-permute-done.4), channel_id=1, source_target_pairs={{0,28},{4,0},{8,4},{12,8},{16,12},{20,16},{24,20},{28,24},{1,29},{... | collective-permute-start | bytes 98312 | tf_op jit(solution)/shard_map/ppermute | solution.py:119
  165.9 1.3 collective-permute-done.1
  167.8 4.7 %collective-permute-start.6 = (bf16[2,8192]{1,0:T(2,128)(2,1)S(1)}, bf16[2,8192]{1,0:T(2,128)(2,1)S(1)}, u32[]{:S(2)}, u32[]{:S(2)}) collective-permute-start(bf16[2,8192]{1,0:T(2,128)(2,1)S(1)} %collective-permute-done.5), channel_id=1, source_target_pairs={{0,28},{4,0},{8,4},{12,8},{16,12},{20,16},{24,20},{28,24},{1,29},{... | collective-permute-start | bytes 98312 | tf_op jit(solution)/shard_map/ppermute | solution.py:119
  172.5 1.3 collective-permute-done.2
  173.8 3.2 copy.63
  177.0 4.7 %copy.64 = bf16[3,1,512,1024]{2,3,0,1:T(8,128)(2,1)} copy(bf16[3,1,512,1024]{3,2,1,0:T(8,128)(2,1)} %get-tuple-element.186) | data formatting | bytes 6291456
  181.7 3.4 concatenate.6
  185.1 1.1 constant_dynamic-slice_fusion.1
  186.1 1.2 gather_fusion
  187.4 1.5 fusion.47
  189.2 58.3 %all_gather.26 = f32[4,3,64]{2,1,0:T(4,128)S(1)} all-gather(f32[1,3,64]{2,1,0:T(4,128)S(1)} %all_gather_reshape.9), channel_id=1, replica_groups=mesh['group'=8,'tp'=4] {'tp'}, dimensions={0}, use_global_device_ids=true | all-gather | bytes 3840 | tf_op jit(solution)/shard_map/all_gather | solution.py:13
  247.5 5.3 %all_gather.27 = f32[4,3,64]{2,1,0:T(4,128)S(1)} all-gather(f32[1,3,64]{2,1,0:T(4,128)S(1)} %all_gather_reshape.10), channel_id=1, replica_groups=mesh['group'=8,'tp'=4] {'tp'}, dimensions={0}, use_global_device_ids=true | all-gather | bytes 3840 | tf_op jit(solution)/shard_map/all_gather | solution.py:13
  252.9 2.8 convolution_bitcast_fusion.1
  255.7 6.5 %all_gather.28 = f32[4,3,64,128]{3,2,1,0:T(8,128)S(1)} all-gather(f32[1,3,64,128]{3,2,1,0:T(8,128)S(1)} %convolution_bitcast_fusion.1), channel_id=1, replica_groups=mesh['group'=8,'tp'=4] {'tp'}, dimensions={0}, use_global_device_ids=true | all-gather | bytes 491520 | tf_op jit(solution)/shard_map/all_gather | solution.py:13
  263.0 26.0 %all-gather.1 = f32[8,3,16]{2,1,0:T(4,128)S(1)} all-gather(f32[1,3,16]{2,1,0:T(4,128)S(1)} %dynamic-slice_bitcast_fusion), channel_id=1, replica_groups=mesh['group'=8,'tp'=4] {'group'}, dimensions={0}, use_global_device_ids=true | all-gather | bytes 1728 | tf_op jit(solution)/shard_map/all_gather | solution.py:157
  289.1 26.0 %all-gather = f32[8,3,16]{2,1,0:T(4,128)S(1)} all-gather(f32[1,3,16]{2,1,0:T(4,128)S(1)} %dynamic-slice_bitcast_fusion.1), channel_id=1, replica_groups=mesh['group'=8,'tp'=4] {'group'}, dimensions={0}, use_global_device_ids=true | all-gather | bytes 1728 | tf_op jit(solution)/shard_map/all_gather | solution.py:156
  315.2 30.6 %all_gather.29 = f32[24,16,128]{2,1,0:T(8,128)S(1)} all-gather(f32[3,16,128]{2,1,0:T(8,128)S(1)} %constant_dynamic-slice_fusion), channel_id=1, replica_groups=mesh['group'=8,'tp'=4] {'group'}, dimensions={0}, use_global_device_ids=true | all-gather | bytes 221184 | tf_op jit(solution)/shard_map/all_gather | solution.py:158
  345.8 0.7 select_reduce_fusion
  346.5 0.9 fusion.27
  347.5 1.0 fusion.20
  348.5 5.4 %multiply_reduce_fusion = f32[16,256,128]{2,1,0:T(8,128)S(1)} fusion(f32[4,16,256,128]{3,2,1,0:T(8,128)} %all-to-all-done, f32[4,16,256]{2,1,0:T(8,128)S(1)} %get-tuple-element.181), kind=kLoop, calls=%fused_computation.28 | loop fusion | flops 3670016 | bytes 10551296 | tf_op jit(solution)/shard_map/reduce_sum | solution.py:41
  353.9 0.7 fusion.16
  355.2 1.4 copy.52
  (79 shorter events, 9.7 us)
Async XLA Ops:
  7.2 40.2 %all-gather.4.cloned.1.call-start = ((), (), s32[]{:S(2)}) async-start(), calls=%async_computation.3 | async-start | bytes 5242880 | tf_op jit(solution)/shard_map/all_gather | solution.py:78
  13.6 6.6 %copy-start.6 = (s32[8]{0:T(128)S(1)}, s32[8]{0:T(128)}, u32[]{:S(2)}) copy-start(s32[8]{0:T(128)} %param.13) | copy-start | bytes 100
  47.3 89.8 %copy-start.3 = (bf16[2,2048]{1,0:T(2,128)(2,1)S(1)}, bf16[2,2048]{1,0:T(2,128)(2,1)}, u32[]{:S(2)}) copy-start(bf16[2,2048]{1,0:T(2,128)(2,1)} %param.14) | copy-start | bytes 24580
  47.3 99.8 %copy-start.7 = (s32[24]{0:T(128)S(1)}, s32[24]{0:T(128)}, u32[]{:S(2)}) copy-start(s32[24]{0:T(128)} %param.17) | copy-start | bytes 292
  133.9 13.4 %all-to-all-start.1 = ((f32[4,16,256]{2,1,0:T(8,128)}), f32[4,16,256]{2,1,0:T(8,128)S(1)}, u32[]{:S(2)}, u32[]{:S(2)}) async-start(f32[4,16,256]{2,1,0:T(8,128)} %bitcast.11), calls=%async_computation.1 | async-start | bytes 131072 | tf_op jit(solution)/shard_map/all_to_all | solution.py:92
  142.4 18.1 %collective-permute-start = (bf16[2,8192]{1,0:T(2,128)(2,1)S(1)}, bf16[2,8192]{1,0:T(2,128)(2,1)S(1)}, u32[]{:S(2)}, u32[]{:S(2)}) collective-permute-start(bf16[2,8192]{1,0:T(2,128)(2,1)S(1)} %all_gather.25), channel_id=1, source_target_pairs={{0,4},{4,8},{8,12},{12,16},{16,20},{20,24},{24,28},{28,0},{1,5},{5... | collective-permute-start | bytes 98312 | tf_op jit(solution)/shard_map/ppermute | solution.py:116
  143.9 17.3 %collective-permute-start.4 = (bf16[2,8192]{1,0:T(2,128)(2,1)S(1)}, bf16[2,8192]{1,0:T(2,128)(2,1)S(1)}, u32[]{:S(2)}, u32[]{:S(2)}) collective-permute-start(bf16[2,8192]{1,0:T(2,128)(2,1)S(1)} %all_gather.25), channel_id=1, source_target_pairs={{0,28},{4,0},{8,4},{12,8},{16,12},{20,16},{24,20},{28,24},{1,29},{... | collective-permute-start | bytes 98312 | tf_op jit(solution)/shard_map/ppermute | solution.py:119
  147.2 0.6 copy-start
  147.8 200.6 %all-to-all-start = ((f32[4,16,256,128]{3,2,1,0:T(8,128)}), f32[4,16,256,128]{3,2,1,0:T(8,128)}, u32[]{:S(2)}, u32[]{:S(2)}) async-start(f32[4,16,256,128]{3,2,1,0:T(8,128)} %bitcast.129), calls=%async_computation | async-start | bytes 16777216 | tf_op jit(solution)/shard_map/all_to_all | solution.py:94
  153.6 7.0 %copy-start.5 = (s32[24]{0:T(128)S(1)}, s32[24]{0:T(128)}, u32[]{:S(2)}) copy-start(s32[24]{0:T(128)} %param.16) | copy-start | bytes 292
  160.5 6.7 %collective-permute-start.1 = (bf16[2,8192]{1,0:T(2,128)(2,1)S(1)}, bf16[2,8192]{1,0:T(2,128)(2,1)S(1)}, u32[]{:S(2)}, u32[]{:S(2)}) collective-permute-start(bf16[2,8192]{1,0:T(2,128)(2,1)S(1)} %collective-permute-done), channel_id=1, source_target_pairs={{0,4},{4,8},{8,12},{12,16},{16,20},{20,24},{24,28},{28,0},{1,5},{5... | collective-permute-start | bytes 98312 | tf_op jit(solution)/shard_map/ppermute | solution.py:116
  161.2 6.6 %collective-permute-start.5 = (bf16[2,8192]{1,0:T(2,128)(2,1)S(1)}, bf16[2,8192]{1,0:T(2,128)(2,1)S(1)}, u32[]{:S(2)}, u32[]{:S(2)}) collective-permute-start(bf16[2,8192]{1,0:T(2,128)(2,1)S(1)} %collective-permute-done.4), channel_id=1, source_target_pairs={{0,28},{4,0},{8,4},{12,8},{16,12},{20,16},{24,20},{28,24},{1,29},{... | collective-permute-start | bytes 98312 | tf_op jit(solution)/shard_map/ppermute | solution.py:119
  167.2 6.6 %collective-permute-start.2 = (bf16[2,8192]{1,0:T(2,128)(2,1)S(1)}, bf16[2,8192]{1,0:T(2,128)(2,1)S(1)}, u32[]{:S(2)}, u32[]{:S(2)}) collective-permute-start(bf16[2,8192]{1,0:T(2,128)(2,1)S(1)} %collective-permute-done.1), channel_id=1, source_target_pairs={{0,4},{4,8},{8,12},{12,16},{16,20},{20,24},{24,28},{28,0},{1,5},{5... | collective-permute-start | bytes 98312 | tf_op jit(solution)/shard_map/ppermute | solution.py:116
  167.8 13.9 %collective-permute-start.6 = (bf16[2,8192]{1,0:T(2,128)(2,1)S(1)}, bf16[2,8192]{1,0:T(2,128)(2,1)S(1)}, u32[]{:S(2)}, u32[]{:S(2)}) collective-permute-start(bf16[2,8192]{1,0:T(2,128)(2,1)S(1)} %collective-permute-done.5), channel_id=1, source_target_pairs={{0,28},{4,0},{8,4},{12,8},{16,12},{20,16},{24,20},{28,24},{1,29},{... | collective-permute-start | bytes 98312 | tf_op jit(solution)/shard_map/ppermute | solution.py:119
  173.8 7.9 %collective-permute-start.3 = (bf16[2,8192]{1,0:T(2,128)(2,1)S(1)}, bf16[2,8192]{1,0:T(2,128)(2,1)S(1)}, u32[]{:S(2)}, u32[]{:S(2)}) collective-permute-start(bf16[2,8192]{1,0:T(2,128)(2,1)S(1)} %collective-permute-done.2), channel_id=1, source_target_pairs={{0,4},{4,8},{8,12},{12,16},{16,20},{20,24},{24,28},{28,0},{1,5},{5... | collective-permute-start | bytes 98312 | tf_op jit(solution)/shard_map/ppermute | solution.py:116
  188.9 158.6 %copy-start.4 = (pred[2,24]{1,0:T(4,128)(4,1)S(1)}, pred[2,24]{1,0:T(4,128)(4,1)}, u32[]{:S(2)}) copy-start(pred[2,24]{1,0:T(4,128)(4,1)} %broadcast_compare_fusion.2) | copy-start | bytes 148
  188.9 159.6 %copy-start.1 = (f32[4,16,256]{2,1,0:T(8,128)S(1)}, f32[4,16,256]{2,1,0:T(8,128)}, u32[]{:S(2)}) copy-start(f32[4,16,256]{2,1,0:T(8,128)} %copy-done) | copy-start | bytes 196612
  188.9 159.6 %copy-start.2 = (f32[4,16,256]{2,1,0:T(8,128)S(1)}, f32[4,16,256]{2,1,0:T(8,128)}, u32[]{:S(2)}) copy-start(f32[4,16,256]{2,1,0:T(8,128)} %all_to_all.15) | copy-start | bytes 196612
Sparse Core Ops, SparseCore 0:
  10.1 37.1 all-gather.3
